TPU v7x, 256 devices: a whole 4x4x8 slice. The times are simulated.
256 devices in a mesh: seq: 8 (over z), ch: 32 (over y, x, core).
Axes of the slice: x: 4, y: 4, z: 8, core: 2. Of those that a mesh axis runs over, the one named last changes fastest.
Arguments:
- tokens: bfloat16 [1024, 4096], P('seq', 'ch'), may hold values from -6 to 6
- input_weight: bfloat16 [3, 4096, 4096], P(None, None, 'ch'), may hold values from -0.09375 to 0.09375
- output_weight: bfloat16 [4096, 4096], P('ch'), may hold values from -0.1875 to 0.1875
- filter_first: bfloat16 [64, 1536], P('ch'), may hold values from -1.5 to 1.5, as said below
- filter_second: bfloat16 [64, 1536], P('ch'), may hold values from -1.5 to 1.5, as said below
Outputs:
- output: bfloat16 [1024, 4096], P('seq', 'ch')
- future_first: float32 [512, 4096], P('seq', 'ch')
- future_second: float32 [512, 4096], P('seq', 'ch')
Inputs may be any that keep to these rules, and one draw needn't show every extreme that they name: filter_first holds each head's taps, drawn independently from tap to tap. filter_second holds each head's taps, drawn independently from tap to tap.
All inputs are finite; a program needn't handle non-finite values.
Results may differ from a plain program's by a relative error of at most 0.0076.
Values may be sent and summed in bfloat16 or wider, within the bound.
A program may use at most 64 MiB of HBM per device.

v0:
```python
import jax
import jax.numpy as jnp
from jax import lax
from jax.sharding import PartitionSpec as P


def toeplitz_rows(lag_values, row_count, col_count):
    width = row_count + col_count
    head_count = lag_values.shape[0]
    padded = jnp.concatenate([lag_values, jnp.zeros((head_count, 1), lag_values.dtype)], axis=1)
    flipped = padded[:, ::-1]
    rotated = jnp.concatenate([flipped[:, row_count:], flipped[:, :row_count]], axis=1)
    tiled = jnp.tile(rotated, (1, row_count))[:, : row_count * (width - 1)]
    return tiled.reshape(head_count, row_count, width - 1)[:, :, :col_count]


def conv_block(sources, source_first, target, padded_filter, tok_dev, fut_dev, total_tokens):
    source_rows = sources.shape[0]
    channels = sources.shape[1]
    head_count = padded_filter.shape[0]
    head_width = channels // head_count
    prompt_start = target * tok_dev - source_first - (source_rows - 1) + total_tokens
    prompt_lags = lax.dynamic_slice_in_dim(
        padded_filter, prompt_start, tok_dev + source_rows - 1, 1
    )
    future_start = total_tokens + target * fut_dev - source_first - (source_rows - 1) + total_tokens
    future_lags = lax.dynamic_slice_in_dim(
        padded_filter, future_start, fut_dev + source_rows - 1, 1
    )
    matrix = jnp.concatenate(
        [
            toeplitz_rows(prompt_lags, tok_dev, source_rows),
            toeplitz_rows(future_lags, fut_dev, source_rows),
        ],
        axis=1,
    )
    grouped = sources.reshape(source_rows, head_count, head_width)
    result = jnp.einsum("hrp,phc->rhc", matrix, grouped, preferred_element_type=jnp.float32)
    return result.reshape(tok_dev + fut_dev, channels)


def conv_layer(signal, padded_filter, tok_dev, fut_dev, first_layer):
    seq_count = lax.axis_size("seq")
    total_tokens = tok_dev * seq_count
    my_index = lax.axis_index("seq")
    my_first = my_index * tok_dev
    block_rows = tok_dev + fut_dev
    channels = signal.shape[1]

    def partial_rows(row_count):

        def one_target(offset):
            return conv_block(
                signal, my_first, offset, padded_filter, tok_dev, fut_dev, total_tokens
            )

        blocks = lax.map(one_target, jnp.arange(row_count // block_rows, dtype=jnp.int32))
        return blocks.reshape(row_count, channels)

    if first_layer:
        return lax.psum_scatter(
            partial_rows(lax.axis_size("seq") * block_rows), "seq", scatter_dimension=0, tiled=True
        )
    return lax.psum_scatter(
        partial_rows(lax.axis_size("seq") * block_rows), "seq", scatter_dimension=0, tiled=True
    )


def per_device(tokens, input_weight, output_weight, filter_first, filter_second):
    tok_dev = tokens.shape[0]
    seq_count = lax.axis_size("seq")
    total_tokens = tok_dev * seq_count
    filter_length = filter_first.shape[1]
    fut_dev = (filter_length - total_tokens) // seq_count
    head_count = filter_first.shape[0]
    projected = jnp.einsum(
        "tp,kpc->ktc",
        lax.all_gather(tokens, "ch", axis=1, tiled=True),
        input_weight,
        preferred_element_type=jnp.float32,
    )
    gates = projected.astype(jnp.bfloat16)
    zero_lags = jnp.zeros((head_count, total_tokens), jnp.bfloat16)
    padded_first = jnp.concatenate([zero_lags, filter_first], axis=1)
    padded_second = jnp.concatenate([zero_lags, filter_second], axis=1)
    first = conv_layer(gates[2], padded_first, tok_dev, fut_dev, True)
    mixed_one = (gates[0].astype(jnp.float32) * first[:tok_dev]).astype(jnp.bfloat16)
    second = conv_layer(mixed_one, padded_second, tok_dev, fut_dev, False)
    mixed_two = (gates[1].astype(jnp.float32) * second[:tok_dev]).astype(jnp.bfloat16)
    partial_terms = jnp.dot(mixed_two, output_weight, preferred_element_type=jnp.float32)
    output = lax.psum_scatter(partial_terms, "ch", scatter_dimension=1, tiled=True).astype(
        jnp.bfloat16
    )
    return (output, first[tok_dev:], second[tok_dev:])


def solution(mesh):
    in_specs = (P("seq", "ch"), P(None, None, "ch"), P("ch", None), P("ch", None), P("ch", None))
    out_specs = (P("seq", "ch"), P("seq", "ch"), P("seq", "ch"))
    return jax.shard_map(
        per_device, mesh=mesh, in_specs=in_specs, out_specs=out_specs, check_vma=False
    )
```

profile of v0, /device:TPU:1, one launch (start us, length us, event | category | flops | bytes accessed | tf_op | source)
XLA Modules:
  0.0 311.8 jit_solution(12222777358940860101)
XLA Ops:
  7.2 0.7 all-gather.2.cloned.1.call-update
  8.0 0.8 concatenate.79
  8.8 53.9 %all-gather.2.cloned.1.call-done = bf16[128,4096]{1,0:T(8,128)(2,1)} async-done(((bf16[128,128]{1,0:T(8,128)(2,1)}), bf16[128,4096]{1,0:T(8,128)(2,1)}) %all-gather.2.cloned.1.call-update) | async-done | bytes 1048592 | tf_op jit(solution)/shard_map/all_gather | solution.py:78
  62.7 2.2 fusion.10
  65.0 0.6 copy-done.1
  65.6 0.9 broadcast.57.clone2
  66.6 36.7 %while.30 = (s32[]{:T(128)}, f32[8,192,128]{2,1,0:T(8,128)}, s32[8]{0:T(128)S(1)}, s32[]{:T(128)}, bf16[2,2560]{1,0:T(2,128)(2,1)S(1)}, /*index=5*/bf16[1,128,12...) while((s32[]{:T(128)}, f32[8,192,128]{2,1,0:T(8,128)}, ...), condition=%wide.region_1.2_spmd, body=%wide.region_0.1_spmd.sunk | while | flops 6491663 | bytes 1997349 | solution.py:57
  66.6 0.6 dynamic_slice.73
  69.7 0.4 reshape.112
  70.5 0.7 constant_dynamic-update-slice_fusion.4
  71.1 0.6 dynamic_slice.73
  74.3 0.4 reshape.112
  75.1 0.7 constant_dynamic-update-slice_fusion.4
  75.7 0.6 dynamic_slice.73
  78.9 0.4 reshape.112
  79.6 0.7 constant_dynamic-update-slice_fusion.4
  80.3 0.6 dynamic_slice.73
  83.5 0.4 reshape.112
  84.2 0.7 constant_dynamic-update-slice_fusion.4
  84.9 0.6 dynamic_slice.73
  88.1 0.4 reshape.112
  88.8 0.7 constant_dynamic-update-slice_fusion.4
  89.5 0.6 dynamic_slice.73
  92.7 0.4 reshape.112
  93.4 0.6 constant_dynamic-update-slice_fusion.4
  94.1 0.6 dynamic_slice.73
  97.2 0.4 reshape.112
  98.0 0.6 constant_dynamic-update-slice_fusion.4
  98.6 0.6 dynamic_slice.73
  101.8 0.4 reshape.112
  102.6 0.6 constant_dynamic-update-slice_fusion.4
  103.3 32.1 %reduce-scatter.10.cloned.1.call-done = f32[192,128]{1,0:T(8,128)} async-done(((f32[1536,128]{1,0:T(8,128)}), f32[192,128]{1,0:T(8,128)}) %reduce-scatter.10.cloned.1.call-update) | async-done | bytes 98320
  135.5 0.8 slice.227
  136.4 0.8 fusion.12
  137.2 0.9 broadcast.57.clone
  138.1 36.7 %while.31 = (s32[]{:T(128)}, f32[8,192,128]{2,1,0:T(8,128)}, s32[8]{0:T(128)S(1)}, s32[]{:T(128)}, bf16[2,2560]{1,0:T(2,128)(2,1)S(1)}, /*index=5*/bf16[128,128]...) while((s32[]{:T(128)}, f32[8,192,128]{2,1,0:T(8,128)}, ...), condition=%wide.region_4.5_spmd, body=%wide.region_3.4_spmd.sunk | while | flops 6491663 | bytes 1997349 | solution.py:57
  138.1 0.6 dynamic_slice.76
  141.3 0.4 reshape.114
  142.1 0.7 constant_dynamic-update-slice_fusion.5
  142.7 0.6 dynamic_slice.76
  145.9 0.4 reshape.114
  146.6 0.7 constant_dynamic-update-slice_fusion.5
  147.3 0.6 dynamic_slice.76
  151.2 0.7 constant_dynamic-update-slice_fusion.5
  151.9 0.6 dynamic_slice.76
  155.8 0.7 constant_dynamic-update-slice_fusion.5
  156.5 0.6 dynamic_slice.76
  160.4 0.7 constant_dynamic-update-slice_fusion.5
  161.0 0.6 dynamic_slice.76
  164.2 0.4 reshape.114
  165.0 0.6 constant_dynamic-update-slice_fusion.5
  165.6 0.6 dynamic_slice.76
  168.8 0.4 reshape.114
  169.6 0.6 constant_dynamic-update-slice_fusion.5
  170.2 0.6 dynamic_slice.76
  173.4 0.4 reshape.114
  174.1 0.6 constant_dynamic-update-slice_fusion.5
  174.9 36.6 %reduce-scatter.12.cloned.1.call-done = f32[192,128]{1,0:T(8,128)} async-done(((f32[1536,128]{1,0:T(8,128)}), f32[192,128]{1,0:T(8,128)}) %reduce-scatter.12.cloned.1.call-update) | async-done | bytes 98320
  211.4 0.8 slice.228
  212.3 3.1 fusion.14
  215.4 1.4 slice.229
  216.8 1.4 slice.230
  218.2 85.6 %reduce-scatter.8.cloned.1.call-done = f32[128,128]{1,0:T(8,128)} async-done(((f32[128,4096]{1,0:T(8,128)}), f32[128,128]{1,0:T(8,128)}) %reduce-scatter.8.cloned.1.call-update) | async-done | bytes 65552 | tf_op jit(solution)/shard_map/reduce_scatter | solution.py:91
  303.8 1.5 convert_element_type.35
  (357 shorter events, 26.3 us)
Async XLA Ops:
  7.2 55.6 %copy-start = (bf16[3,4096,128]{2,1,0:T(8,128)(2,1)S(1)}, bf16[3,4096,128]{2,1,0:T(8,128)(2,1)}, u32[]{:S(2)}) copy-start(bf16[3,4096,128]{2,1,0:T(8,128)(2,1)} %param.10) | copy-start | bytes 9437188
  7.2 55.5 %all-gather.2.cloned.1.call-start = ((), (), s32[]{:S(2)}) async-start(), calls=%async_computation.3 | async-start | bytes 1081344 | tf_op jit(solution)/shard_map/all_gather | solution.py:78
  7.9 127.5 %reduce-scatter.10.cloned.1.call-start = ((), (), s32[]{:S(2)}) async-start(), calls=%async_computation.5 | async-start | bytes 884736
  65.0 0.6 copy-start.1
  66.6 36.7 %copy-start.2 = (bf16[2,1536]{1,0:T(2,128)(2,1)S(1)}, bf16[2,1536]{1,0:T(2,128)(2,1)}, u32[]{:S(2)}) copy-start(bf16[2,1536]{1,0:T(2,128)(2,1)} %param.13) | copy-start | bytes 18436
  103.2 108.2 %reduce-scatter.12.cloned.1.call-start = ((), (), s32[]{:S(2)}) async-start(), calls=%async_computation.6 | async-start | bytes 884736
  174.8 129.0 %reduce-scatter.8.cloned.1.call-start = ((), (), s32[]{:S(2)}) async-start(), calls=%async_computation.4 | async-start | bytes 2162688 | tf_op jit(solution)/shard_map/reduce_scatter | solution.py:91
Sparse Core Ops, SparseCore 0:
  10.5 52.1 all-gather.1
  103.4 32.0 reduce-scatter.9
  174.9 36.4 reduce-scatter.11
  215.6 88.1 reduce-scatter.7
where the time goes:
time: 313 us; the launch traced here: 312 us
  waiting for transfers between devices  209 us (67%)
  local copies, waits for them, and re-layouts  56.2 us (18%)
  loops' own time  22 us (7%)
  between operations  13.8 us (4%)
  matrix products  8.19 us (3%)
    reduce_scatter x1, waiting for transfers between devices, per_device(): lax.psum_scatter(partial_terms, 'ch', scatter_dimension=1, tiled=True)  85.6 us
    unnamed x6, waiting for transfers between devices  69.4 us
    all_gather x1, waiting for transfers between devices, per_device(): lax.all_gather(tokens, 'ch', axis=1, tiled=True)  53.9 us
    another operation x2, loops' own time, partial_rows(): lax.map(one_target, jnp.arange(row_count // block_rows, dtype=jnp.int32))  22 us
    dynamic_update_slice x32, local copies, waits for them, and re-layouts, partial_rows(): lax.map(one_target, jnp.arange(row_count // block_rows, dtype=jnp.int32))  12 us
    reshape x32, local copies, waits for them, and re-layouts, toeplitz_rows(): return tiled.reshape(head_count, row_count, width - 1)[:, :, :col_count]  10.3 us
    dynamic_slice x16, local copies, waits for them, and re-layouts, partial_rows(): lax.map(one_target, jnp.arange(row_count // block_rows, dtype=jnp.int32))  9.31 us
  transfers between devices with their start and end apart: 4, of which 4 were waited for; matrix products, arithmetic and copies ran while one was open for 1% of the time, Pallas kernels for 0%

commit v1 on v0

v1 whole, which is shorter than its diff:
```python
import functools

import jax
import jax.numpy as jnp
from jax import lax
from jax.experimental import pallas as pl
from jax.experimental.pallas import tpu as pltpu
from jax.sharding import PartitionSpec as P

MESH = pl.DeviceIdType.MESH
B = 128
H = 64
F32 = jnp.float32
BF16 = jnp.bfloat16


def build_toeplitz(taps, matrix):
    width = taps.shape[1] + B
    padded = jnp.concatenate([jnp.zeros((1, B), F32), taps], axis=1)
    rows = jnp.broadcast_to(padded, (8, width))
    row = lax.broadcasted_iota(jnp.int32, (8, width), 0)
    for bit in (1, 2, 4):
        rows = jnp.where((row & bit) != 0, pltpu.roll(rows, bit, 1), rows)
    for pair in range(B // 16):
        low = rows if pair == 0 else pltpu.roll(rows, 16 * pair, 1)
        high = pltpu.roll(rows, 16 * pair + 8, 1)
        both = jnp.concatenate([low[:, B:], high[:, B:]], axis=0)
        matrix[16 * pair : 16 * pair + 16, :] = both.astype(BF16)


def kernel(
    q, nz, copies,
    tok, wi, wo, f1, f2,
    out, ff, fs,
    X, Wv, Wc, acc, F1v, F2v, M1, M2, S1, G, P1, P2, U2, S2, V,
    FS1, FS2, FL1, FL2, PS, OA, OB, RA, RB, QA, QB, RA2, RB2,
    ssem, rsem, lsem,
):
    cz = B // nz
    prompt = nz
    blocks = M1.shape[1] // B
    z = lax.axis_index("seq")
    ch = lax.axis_index("ch")
    core = ch % 2
    x = (ch // 2) % q
    y = ch // (2 * q)

    def ch_of(yy, xx, cc):
        return (yy * q + xx) * 2 + cc

    def xpeer(e):
        return (z, ch_of(y, (x + e) % q, core))

    def ypeer(e):
        return (z, ch_of((y + e) % q, x, core))

    sibling = (z, ch_of(y, x, 1 - core))

    def zpeer(e, cc):
        return ((z + e) % nz, ch_of(y, x, cc))

    counter = [0]
    sent = []

    def send(src, dst, device):
        i = counter[0]
        counter[0] += 1
        copy = pltpu.make_async_remote_copy(
            src_ref=src, dst_ref=dst, send_sem=ssem.at[i], recv_sem=rsem.at[i],
            device_id=device, device_id_type=MESH,
        )
        copy.start()
        sent.append(copy)
        return copy

    local_count = [0]

    def local(src, dst):
        i = local_count[0]
        local_count[0] += 1
        copy = pltpu.make_async_copy(src, dst, lsem.at[i])
        copy.start()
        return copy

    barrier = pltpu.get_barrier_semaphore()
    partners = [sibling]
    for e in range(1, q):
        partners += [xpeer(e), ypeer(e)]
    for e in range(1, nz):
        partners += [zpeer(e, core), zpeer(e, 1 - core)]
    for device in partners:
        pl.semaphore_signal(barrier, inc=1, device_id=device, device_id_type=MESH)

    own = local(tok, X.at[0, 0, 0])
    taps = [local(f1, F1v), local(f2, F2v)]
    weights = []
    for k in (2, 0, 1):
        for r in range(2):
            weights.append(
                local(
                    wi.at[k, :, core if r == 0 else 1 - core],
                    Wv.at[:, r, :, ((k + 1) % 3) * B : ((k + 1) % 3) * B + B],
                )
            )
    outw = []
    for c in range(q * q):
        outw.append(
            local(wo.at[:, pl.ds(pl.multiple_of((2 * c + core) * B, B), B)], Wc.at[c, 0])
        )
    pl.semaphore_wait(barrier, len(partners))

    ag_x = [send(tok, X.at[0, q - e, 0], xpeer(e)) for e in range(1, q)]
    ag_y = [send(tok, X.at[q - e, 0, 0], ypeer(e)) for e in range(1, q)]
    ag_s = [send(tok, X.at[0, 0, 1], sibling)]
    wo_s = []

    own.wait()
    for copy in taps:
        copy.wait()
    first_head = z * cz < H

    def head_taps(ref):
        both = ref[...].astype(F32)
        return jnp.where(first_head, both[0:1], both[1:2])

    build_toeplitz(head_taps(F1v), M1)

    for copy in ag_x:
        copy.wait_recv()
    ag_a = [
        send(X.at[0, 1:q, 0, 0:H], X.at[q - e, 1:q, 0, 0:H], ypeer(e)) for e in range(1, q)
    ]
    for copy in ag_y:
        copy.wait_recv()
    ag_b = [
        send(X.at[1:q, 0, 0, H:B], X.at[1:q, q - e, 0, H:B], xpeer(e)) for e in range(1, q)
    ]
    ag_s.append(send(X.at[0, 1:q, 0], X.at[0, 1:q, 1], sibling))
    ag_s.append(send(X.at[1:q, 0, 0], X.at[1:q, 0, 1], sibling))

    for c in range(q * q):
        wo_s.append(
            send(
                wo.at[:, pl.ds(pl.multiple_of((2 * c + 1 - core) * B, B), B)],
                Wc.at[c, 1],
                sibling,
            )
        )

    build_toeplitz(head_taps(F2v), M2)
    for copy in weights:
        copy.wait()

    def chip_of(dy, dx):
        return ((y + dy) % q) * q + (x + dx) % q

    def terms(dy, dx, cols):
        tile = jnp.concatenate([X[dy, dx, 0], X[dy, dx, 1]], axis=1)
        c = chip_of(dy, dx)
        weight = jnp.concatenate([Wv[c, 0, :, cols], Wv[c, 1, :, cols]], axis=0)
        return jnp.dot(tile, weight, preferred_element_type=F32)

    every = slice(0, 3 * B)
    for copy in ag_s:
        copy.wait_recv()
    total = terms(0, 0, every)
    for d in range(1, q):
        total += terms(0, d, every)
        total += terms(d, 0, every)
    acc[...] = total

    for e in range(1, q):
        ag_a[e - 1].wait_recv()
        ag_s.append(send(X.at[q - e, 1:q, 0, 0:H], X.at[q - e, 1:q, 1, 0:H], sibling))
        ag_b[e - 1].wait_recv()
        ag_s.append(send(X.at[1:q, q - e, 0, H:B], X.at[1:q, q - e, 1, H:B], sibling))
    for copy in ag_s[3:]:
        copy.wait_recv()

    a2a = []
    for part in range(3):
        cols = slice(part * B, part * B + B)
        total = acc[:, cols]
        for dy in range(1, q):
            for dx in range(1, q):
                total += terms(dy, dx, cols)
        flipped = jnp.transpose(total).astype(BF16)
        S1[part] = flipped.reshape(nz, cz, B)
        for e in range(1, nz):
            a2a.append(
                send(S1.at[part, (z + e) % nz], G.at[part, z], zpeer(e, core))
            )
        G[part, z] = S1[part, z]

    def received(part):
        for copy in a2a[part * (nz - 1) : (part + 1) * (nz - 1)]:
            copy.wait_recv()

    def conv_block(P_ref, t):
        total = None
        for s in range(nz):
            if 0 <= t - s < blocks:
                term = P_ref[s * cz : s * cz + cz, (t - s) * B : (t - s) * B + B]
                total = term if total is None else total + term
        return total

    received(0)
    signal = G[0].reshape(B, B)
    P1[:, : prompt * B] = jnp.dot(signal, M1[:, : prompt * B], preferred_element_type=F32)
    received(1)
    for t in range(prompt):
        mixed = (G[1, t].astype(F32) * conv_block(P1, t)).astype(BF16)
        U2[t * cz : t * cz + cz, :] = mixed
    P2[:, : prompt * B] = jnp.dot(U2[...], M2[:, : prompt * B], preferred_element_type=F32)
    received(2)
    for t in range(prompt):
        S2[t] = (G[2, t].astype(F32) * conv_block(P2, t)).astype(BF16)
    back = []
    for e in range(1, nz):
        back.append(send(S2.at[(z + e) % nz], V.at[0, z], zpeer(e, core)))
        back.append(send(S2.at[(z + e) % nz], V.at[1, z], zpeer(e, 1 - core)))
    back.append(send(S2.at[z], V.at[1, z], sibling))
    V[0, z] = S2[z]

    future = []
    for P_ref, M_ref, sig, FS, FL in ((P1, M1, signal, FS1, FL1), (P2, M2, U2[...], FS2, FL2)):
        P_ref[:, prompt * B :] = jnp.dot(sig, M_ref[:, prompt * B :], preferred_element_type=F32)
        for t in range(prompt, blocks):
            FS[t - prompt] = conv_block(P_ref, t)
        group = []
        for e in range(1, nz):
            group.append(send(FS.at[((z + e) % nz) // 2], FL.at[z], zpeer(e, core)))
        FL[z] = FS[z // 2]
        future.append(group)

    for copy in outw:
        copy.wait()
    for copy in wo_s:
        copy.wait_recv()
    for copy in back:
        copy.wait_recv()
    mixed = jnp.transpose(V[...].reshape(2 * B, B).astype(F32)).astype(BF16)
    for dx in list(range(1, q)) + [0]:
        for dy in range(q):
            c = chip_of(dy, dx)
            weight = jnp.concatenate([Wc[c, 0], Wc[c, 1]], axis=0)
            block = jnp.dot(mixed, weight, preferred_element_type=F32)
            PS[dy, dx] = block.astype(BF16)
            if dx == 0:
                OA[dy] = block[0:H]
            if dy == 0:
                OB[dx] = block[H:B]
    rs_a = [send(PS.at[:, e, 0:H], RA.at[q - e], xpeer(e)) for e in range(1, q)]
    rs_b = [send(PS.at[e, :, H:B], RB.at[q - e], ypeer(e)) for e in range(1, q)]

    def future_rows(group, FL, ref):
        for copy in group:
            copy.wait_recv()
        rows = jnp.transpose(FL[...].reshape(B, B))
        ref[...] = jnp.where(z % 2 == 0, rows[0:H], rows[H:B])

    future_rows(future[0], FL1, ff)
    future_rows(future[1], FL2, fs)

    for copy in rs_a:
        copy.wait_recv()
    for d in range(q):
        total = OA[d]
        for e in range(1, q):
            total += RA[e, d].astype(F32)
        OA[d] = total
        QA[d] = total.astype(BF16)
    rs_a2 = [send(QA.at[e], RA2.at[q - e], ypeer(e)) for e in range(1, q)]
    for copy in rs_b:
        copy.wait_recv()
    for d in range(q):
        total = OB[d]
        for e in range(1, q):
            total += RB[e, d].astype(F32)
        OB[d] = total
        QB[d] = total.astype(BF16)
    rs_b2 = [send(QB.at[e], RB2.at[q - e], xpeer(e)) for e in range(1, q)]

    for group, O, R, rows in ((rs_a2, OA, RA2, slice(0, H)), (rs_b2, OB, RB2, slice(H, B))):
        for copy in group:
            copy.wait_recv()
        total = O[0]
        for e in range(1, q):
            total += R[e].astype(F32)
        out[rows, :] = total.astype(BF16)

    for copy in sent:
        copy.wait_send()
    assert counter[0] == copies, counter[0]


def per_device(nz, tokens, input_weight, output_weight, filter_first, filter_second):
    depth, width = input_weight.shape[1:]
    chips = depth // (2 * B)
    q = int(round(chips**0.5))
    cz = B // nz
    taps = filter_first.shape[1]
    future = (taps // B - nz)
    copies = 4 * (q - 1) + 3 + q * q + 2 * (q - 1) + 3 * (nz - 1)
    copies += 2 * (nz - 1) + 1 + 2 * (nz - 1) + 4 * (q - 1)
    weights = input_weight.reshape(3, chips, 2, B, width)
    hbm = pl.BlockSpec(memory_space=pl.ANY)
    vmem = pl.BlockSpec(memory_space=pltpu.VMEM)
    scratch = [
        pltpu.VMEM((q, q, 2, B, B), BF16),
        pltpu.VMEM((chips, 2, B, 3 * B), BF16),
        pltpu.VMEM((chips, 2, B, B), BF16),
        pltpu.VMEM((B, 3 * B), F32),
        pltpu.VMEM((2, taps), BF16),
        pltpu.VMEM((2, taps), BF16),
        pltpu.VMEM((B, taps), BF16),
        pltpu.VMEM((B, taps), BF16),
        pltpu.VMEM((3, nz, cz, B), BF16),
        pltpu.VMEM((3, nz, cz, B), BF16),
        pltpu.VMEM((B, taps), F32),
        pltpu.VMEM((B, taps), F32),
        pltpu.VMEM((B, B), BF16),
        pltpu.VMEM((nz, cz, B), BF16),
        pltpu.VMEM((2, nz, cz, B), BF16),
        pltpu.VMEM((future, cz, B), F32),
        pltpu.VMEM((future, cz, B), F32),
        pltpu.VMEM((nz, cz, B), F32),
        pltpu.VMEM((nz, cz, B), F32),
        pltpu.VMEM((q, q, B, B), BF16),
        pltpu.VMEM((q, H, B), F32),
        pltpu.VMEM((q, H, B), F32),
        pltpu.VMEM((q, q, H, B), BF16),
        pltpu.VMEM((q, q, H, B), BF16),
        pltpu.VMEM((q, H, B), BF16),
        pltpu.VMEM((q, H, B), BF16),
        pltpu.VMEM((q, H, B), BF16),
        pltpu.VMEM((q, H, B), BF16),
        pltpu.SemaphoreType.DMA((copies,)),
        pltpu.SemaphoreType.DMA((copies,)),
        pltpu.SemaphoreType.DMA((9 + chips,)),
    ]
    return pl.pallas_call(
        functools.partial(kernel, q, nz, copies),
        out_shape=(
            jax.ShapeDtypeStruct((B, B), BF16),
            jax.ShapeDtypeStruct((H, B), F32),
            jax.ShapeDtypeStruct((H, B), F32),
        ),
        in_specs=[hbm] * 5,
        out_specs=(vmem, vmem, vmem),
        scratch_shapes=scratch,
        compiler_params=pltpu.CompilerParams(
            collective_id=0, has_side_effects=True, vmem_limit_bytes=32 * 2**20
        ),
    )(tokens, weights, output_weight, filter_first, filter_second)


def solution(mesh):
    in_specs = (P("seq", "ch"), P(None, None, "ch"), P("ch", None), P("ch", None), P("ch", None))
    out_specs = (P("seq", "ch"), P("seq", "ch"), P("seq", "ch"))
    return jax.shard_map(
        functools.partial(per_device, mesh.shape["seq"]),
        mesh=mesh, in_specs=in_specs, out_specs=out_specs, check_vma=False,
    )
```

time: 313 us -> 50.5 us (0.16)
  waiting for transfers between devices: 209 us -> 0 us
  local copies, waits for them, and re-layouts: 56.2 us -> 7.09 us
  Pallas kernels: 0 us -> 42.4 us
  loops' own time: 22 us -> 0 us
  between operations: 13.8 us -> 0.65 us
  matrix products: 8.19 us -> 0 us
    reduce_scatter x1 -> x0, waiting for transfers between devices: 85.6 us -> none  [per_device(): lax.psum_scatter(partial_terms, 'ch', scatter_dimension=1, tiled=True)]
    unnamed x6 -> x0, waiting for transfers between devices: 69.4 us -> none
    all_gather x1 -> x0, waiting for transfers between devices: 53.9 us -> none  [per_device(): lax.all_gather(tokens, 'ch', axis=1, tiled=True)]
    pallas_call x0 -> x1, Pallas kernels: none -> 42.4 us  [per_device(): pl.pallas_call(functools.partial(kernel, q, nz, copies), out_shape=(jax.S...]
    another operation x2 -> x0, loops' own time: 22 us -> none  [partial_rows(): lax.map(one_target, jnp.arange(row_count // block_rows, dtype=jnp.int32))]
    slice x165 -> x0, local copies, waits for them, and re-layouts: 13.9 us -> none  [the longest x48 4.35 us: toeplitz_rows(): flipped[:, row_count:]]
    dynamic_update_slice x32 -> x0, local copies, waits for them, and re-layouts: 12 us -> none  [partial_rows(): lax.map(one_target, jnp.arange(row_count // block_rows, dtype=jnp.int32))]
    dynamic_slice x48 -> x0, local copies, waits for them, and re-layouts: 11.9 us -> none  [the longest x16 9.31 us: partial_rows(): lax.map(one_target, jnp.arange(row_count // block_rows, dtype=jnp.int32))]
  transfers between devices with their start and end apart: 4 -> 0, of which waited for: 4 -> 0; matrix products, arithmetic and copies ran while one was open for 1% -> 0% of each run, Pallas kernels for 0% -> 0%
where the time goes in v1:
time: 50.5 us; the launch traced here: 50.2 us
  Pallas kernels  42.4 us (84%)
  local copies, waits for them, and re-layouts  7.09 us (14%)
  between operations  0.65 us (1%)
    pallas_call x1, Pallas kernels, per_device(): pl.pallas_call(functools.partial(kernel, q, nz, copies), out_shape=(jax.S...  42.4 us
    unnamed x13, local copies, waits for them, and re-layouts  7.09 us

profile of v1, /device:TPU:1, one launch (start us, length us, event | category | flops | bytes accessed | tf_op | source)
XLA Modules:
  0.0 50.2 jit_solution(1248709585797462123)
XLA Ops:
  0.6 0.0 copy-start
  0.6 1.9 %copy-done = bf16[3,4096,128]{2,1,0:T(8,128)(2,1)S(1)} copy-done((bf16[3,4096,128]{2,1,0:T(8,128)(2,1)S(1)}, bf16[3,4096,128]{2,1,0:T(8,128)(2,1)}, u32[]{:S(2)}) %copy-start) | copy-done | bytes 3145752
  2.5 0.0 copy-start.1
  2.5 1.2 %copy-done.1 = bf16[128,4096]{1,0:T(8,128)(2,1)S(1)} copy-done((bf16[128,4096]{1,0:T(8,128)(2,1)S(1)}, bf16[128,4096]{1,0:T(8,128)(2,1)}, u32[]{:S(2)}) %copy-start.1) | copy-done | bytes 1048600
  3.7 0.0 copy-start.2
  3.7 0.8 %copy-done.2 = bf16[128,128]{1,0:T(8,128)(2,1)S(1)} copy-done((bf16[128,128]{1,0:T(8,128)(2,1)S(1)}, bf16[128,128]{1,0:T(8,128)(2,1)}, u32[]{:S(2)}) %copy-start.2) | copy-done | bytes 32792
  4.5 0.0 copy-start.3
  4.5 0.7 %copy-done.3 = bf16[2,1536]{1,0:T(2,128)(2,1)S(1)} copy-done((bf16[2,1536]{1,0:T(2,128)(2,1)S(1)}, bf16[2,1536]{1,0:T(2,128)(2,1)}, u32[]{:S(2)}) %copy-start.3) | copy-done | bytes 6168
  5.2 0.0 copy-start.4
  5.2 0.7 %copy-done.4 = bf16[2,1536]{1,0:T(2,128)(2,1)S(1)} copy-done((bf16[2,1536]{1,0:T(2,128)(2,1)S(1)}, bf16[2,1536]{1,0:T(2,128)(2,1)}, u32[]{:S(2)}) %copy-start.4) | copy-done | bytes 6168
  5.9 42.4 %shard_map.76 = (bf16[128,128]{1,0:T(8,128)(2,1)S(1)}, f32[64,128]{1,0:T(8,128)S(1)}, f32[64,128]{1,0:T(8,128)S(1)}) custom-call(bf16[128,128]{1,0:T(8,128)(2,1)S(1)} %copy-done.2, bf16[3,16,2,128,128]{4,3,2,1,0:T(8,128)(2,1)S(1)} %bitcast.1, bf16[128,4096]{1,0:T(8,128)(2,1)S(1)} %copy-done.1, bf16[2,1536]{1,0:T(2,128)(2,1)S(1)} %copy-done.3, ...), custom_call_target="tpu_custom_call" | custom-call | tf_op jit(solution)/shard_map/pallas_call | solution.py:342
  48.3 0.6 %copy.11 = bf16[128,128]{1,0:T(8,128)(2,1)} copy(bf16[128,128]{1,0:T(8,128)(2,1)S(1)} %get-tuple-element.6) | data formatting | bytes 65536
  48.9 0.6 %copy.12 = f32[64,128]{1,0:T(8,128)} copy(f32[64,128]{1,0:T(8,128)S(1)} %get-tuple-element.7) | data formatting | bytes 65536
  49.5 0.6 %copy.13 = f32[64,128]{1,0:T(8,128)} copy(f32[64,128]{1,0:T(8,128)S(1)} %get-tuple-element.8) | data formatting | bytes 65536
Async XLA Ops:
  0.6 1.9 %copy-start = (bf16[3,4096,128]{2,1,0:T(8,128)(2,1)S(1)}, bf16[3,4096,128]{2,1,0:T(8,128)(2,1)}, u32[]{:S(2)}) copy-start(bf16[3,4096,128]{2,1,0:T(8,128)(2,1)} %param.6) | copy-start | bytes 9437188
  2.5 1.2 %copy-start.1 = (bf16[128,4096]{1,0:T(8,128)(2,1)S(1)}, bf16[128,4096]{1,0:T(8,128)(2,1)}, u32[]{:S(2)}) copy-start(bf16[128,4096]{1,0:T(8,128)(2,1)} %wo.1) | copy-start | bytes 3145732
  3.7 0.8 %copy-start.2 = (bf16[128,128]{1,0:T(8,128)(2,1)S(1)}, bf16[128,128]{1,0:T(8,128)(2,1)}, u32[]{:S(2)}) copy-start(bf16[128,128]{1,0:T(8,128)(2,1)} %tok.1) | copy-start | bytes 98308
  4.5 0.7 %copy-start.3 = (bf16[2,1536]{1,0:T(2,128)(2,1)S(1)}, bf16[2,1536]{1,0:T(2,128)(2,1)}, u32[]{:S(2)}) copy-start(bf16[2,1536]{1,0:T(2,128)(2,1)} %f1.1) | copy-start | bytes 18436
  5.2 0.7 %copy-start.4 = (bf16[2,1536]{1,0:T(2,128)(2,1)S(1)}, bf16[2,1536]{1,0:T(2,128)(2,1)}, u32[]{:S(2)}) copy-start(bf16[2,1536]{1,0:T(2,128)(2,1)} %f2.1) | copy-start | bytes 18436

commit v2 on v1

v2 whole, which is shorter than its diff:
```python
import functools

import jax
import jax.numpy as jnp
from jax import lax
from jax.experimental import pallas as pl
from jax.experimental.pallas import tpu as pltpu
from jax.sharding import PartitionSpec as P

MESH = pl.DeviceIdType.MESH
B = 128
H = 64
F32 = jnp.float32
BF16 = jnp.bfloat16


def build_toeplitz(taps, matrix):
    width = taps.shape[1] + B
    padded = jnp.concatenate([jnp.zeros((1, B), F32), taps], axis=1)
    rows = jnp.broadcast_to(padded, (8, width))
    row = lax.broadcasted_iota(jnp.int32, (8, width), 0)
    for bit in (1, 2, 4):
        rows = jnp.where((row & bit) != 0, pltpu.roll(rows, bit, 1), rows)
    for pair in range(B // 16):
        low = rows if pair == 0 else pltpu.roll(rows, 16 * pair, 1)
        high = pltpu.roll(rows, 16 * pair + 8, 1)
        both = jnp.concatenate([low[:, B:], high[:, B:]], axis=0)
        matrix[16 * pair : 16 * pair + 16, :] = both.astype(BF16)


def kernel(
    q, nz, copies,
    tok, wi, wo, f1, f2,
    out, ff, fs,
    X, Wv, Wc, acc, F1v, F2v, M1, M2, S0, S1, G0, G1, P1, P2, U2, S2, V,
    FS1, FS2, FL1, FL2, PS, OA, OB, RA, RB, QA, QB, RA2, RB2,
    ssem, rsem, lsem,
):
    cz = B // nz
    prompt = nz
    blocks = M1.shape[1] // B
    z = lax.axis_index("seq")
    ch = lax.axis_index("ch")
    core = ch % 2
    x = (ch // 2) % q
    y = ch // (2 * q)

    near = [1, q - 1] if q > 2 else [1]
    offsets = [0] + near + [e for e in range(2, q - 1)]
    slot_of = {e: i for i, e in enumerate(offsets)}
    groups = [(1, 1 + len(near))] + [(i, i + 1) for i in range(1 + len(near), q)]
    steps = offsets[1:]

    def land(e):
        return slot_of[q - e]

    def ch_of(yy, xx, cc):
        return (yy * q + xx) * 2 + cc

    def xpeer(e):
        return (z, ch_of(y, (x + e) % q, core))

    def ypeer(e):
        return (z, ch_of((y + e) % q, x, core))

    sibling = (z, ch_of(y, x, 1 - core))

    def zpeer(e):
        return ((z + e) % nz, ch)

    far_first = sorted(range(1, nz), key=lambda e: -min(e, nz - e))
    near_first = sorted(range(1, nz), key=lambda e: min(e, nz - e))

    counter = [0]
    sent = []

    def send(src, dst, device):
        i = counter[0]
        counter[0] += 1
        copy = pltpu.make_async_remote_copy(
            src_ref=src, dst_ref=dst, send_sem=ssem.at[i], recv_sem=rsem.at[i],
            device_id=device, device_id_type=MESH,
        )
        copy.start()
        sent.append(copy)
        return copy

    local_count = [0]

    def local(src, dst):
        i = local_count[0]
        local_count[0] += 1
        copy = pltpu.make_async_copy(src, dst, lsem.at[i])
        copy.start()
        return copy

    barrier = pltpu.get_barrier_semaphore()
    partners = [zpeer(e) for e in far_first]
    for e in range(1, q):
        partners += [xpeer(e), ypeer(e)]
    partners.append(sibling)
    for device in partners:
        pl.semaphore_signal(barrier, inc=1, device_id=device, device_id_type=MESH)

    own = local(tok, X.at[0, 0, 0])
    taps = [local(f1, F1v), local(f2, F2v)]
    weights = []
    for k, column in ((2, 0), (0, 1), (1, 2)):
        for r in range(2):
            weights.append(
                local(
                    wi.at[k, :, core if r == 0 else 1 - core],
                    Wv.at[:, r, :, column * B : column * B + B],
                )
            )
    pl.semaphore_wait(barrier, len(partners))

    ag_x, ag_y = {}, {}
    for e in steps:
        ag_x[e] = send(tok, X.at[0, land(e), 0], xpeer(e))
        ag_y[e] = send(tok, X.at[land(e), 0, 0], ypeer(e))
    sib_own = send(tok, X.at[0, 0, 1], sibling)

    first_head = z * cz < H

    def head_taps(ref):
        both = ref[...].astype(F32)
        return jnp.where(first_head, both[0:1], both[1:2])

    for copy in taps:
        copy.wait()
    build_toeplitz(head_taps(F1v), M1)

    sib_x, sib_y, ag_a, ag_b = [], [], [], []
    for g, (lo, hi) in enumerate(groups):
        for e in range(1, q):
            if lo <= land(e) < hi:
                ag_x[e].wait_recv()
        ag_a.append(
            {e: send(X.at[0, lo:hi, 0, 0:H], X.at[land(e), lo:hi, 0, 0:H], ypeer(e)) for e in steps}
        )
        for e in range(1, q):
            if lo <= land(e) < hi:
                ag_y[e].wait_recv()
        ag_b.append(
            {e: send(X.at[lo:hi, 0, 0, H:B], X.at[lo:hi, land(e), 0, H:B], xpeer(e)) for e in steps}
        )
        sib_x.append(send(X.at[0, lo:hi, 0], X.at[0, lo:hi, 1], sibling))
        sib_y.append(send(X.at[lo:hi, 0, 0], X.at[lo:hi, 0, 1], sibling))
        if g == 0:
            build_toeplitz(head_taps(F2v), M2)

    def chip_of(dy, dx):
        return ((y + offsets[dy]) % q) * q + (x + offsets[dx]) % q

    def terms(dy, dx, lo, hi):
        tile = jnp.concatenate([X[dy, dx, 0], X[dy, dx, 1]], axis=1)
        c = chip_of(dy, dx)
        weight = jnp.concatenate([Wv[c, 0, :, lo:hi], Wv[c, 1, :, lo:hi]], axis=0)
        return jnp.dot(tile, weight, preferred_element_type=F32)

    def forward(g, e):
        lo, hi = groups[g]
        s = land(e)
        ag_a[g][e].wait_recv()
        a = send(X.at[s, lo:hi, 0, 0:H], X.at[s, lo:hi, 1, 0:H], sibling)
        ag_b[g][e].wait_recv()
        b = send(X.at[lo:hi, s, 0, H:B], X.at[lo:hi, s, 1, H:B], sibling)
        return [a, b]

    early = list(range(1, 1 + len(near)))
    late = list(range(1 + len(near), q))
    near_e = [e for e in range(1, q) if land(e) in early]
    far_e = [e for e in range(1, q) if land(e) in late]

    own.wait()
    for copy in weights:
        copy.wait()
    sib_own.wait_recv()
    total = terms(0, 0, 0, 3 * B)
    sib_x[0].wait_recv()
    sib_y[0].wait_recv()
    for d in early:
        total += terms(0, d, 0, 3 * B)
        total += terms(d, 0, 0, 3 * B)
    acc[...] = total
    first_fwd = []
    for e in near_e:
        first_fwd += forward(0, e)
    last_fwd = []
    for g, es in [(0, far_e)] + [(g, near_e + far_e) for g in range(1, len(groups))]:
        for e in es:
            last_fwd += forward(g, e)
    total = acc[...]
    for g in range(1, len(groups)):
        sib_x[g].wait_recv()
        sib_y[g].wait_recv()
        for d in range(*groups[g]):
            total += terms(0, d, 0, 3 * B)
            total += terms(d, 0, 0, 3 * B)
    for copy in first_fwd:
        copy.wait_recv()
    for dy in early:
        for dx in early:
            total += terms(dy, dx, 0, 3 * B)
    acc[...] = total
    for copy in last_fwd:
        copy.wait_recv()

    rest = [(dy, dx) for dy in range(1, q) for dx in range(1, q) if dy in late or dx in late]
    total = acc[:, 0:B]
    for dy, dx in rest:
        total += terms(dy, dx, 0, B)
    S0[...] = jnp.transpose(total).astype(BF16).reshape(nz, cz, B)
    a2a_value = [send(S0.at[(z + e) % nz], G0.at[z], zpeer(e)) for e in far_first]
    G0[z] = S0[z]
    total = acc[:, B : 3 * B]
    for dy, dx in rest:
        total += terms(dy, dx, B, 3 * B)
    for part in range(2):
        flipped = jnp.transpose(total[:, part * B : part * B + B])
        S1[:, part] = flipped.astype(BF16).reshape(nz, cz, B)
    a2a_gates = [send(S1.at[(z + e) % nz], G1.at[z], zpeer(e)) for e in far_first]
    G1[z] = S1[z]

    outw, wo_s = [], []
    for c in range(q * q):
        outw.append(
            local(wo.at[:, pl.ds(pl.multiple_of((2 * c + core) * B, B), B)], Wc.at[c, 0])
        )
        wo_s.append(
            send(
                wo.at[:, pl.ds(pl.multiple_of((2 * c + 1 - core) * B, B), B)],
                Wc.at[c, 1],
                sibling,
            )
        )

    def conv_block(P_ref, t):
        total = None
        for s in range(nz):
            if 0 <= t - s < blocks:
                term = P_ref[s * cz : s * cz + cz, (t - s) * B : (t - s) * B + B]
                total = term if total is None else total + term
        return total

    for copy in a2a_value:
        copy.wait_recv()
    signal = G0[...].reshape(B, B)
    P1[:, : prompt * B] = jnp.dot(signal, M1[:, : prompt * B], preferred_element_type=F32)
    for copy in a2a_gates:
        copy.wait_recv()
    for t in range(prompt):
        mixed = (G1[t, 0].astype(F32) * conv_block(P1, t)).astype(BF16)
        U2[t * cz : t * cz + cz, :] = mixed
    P2[:, : prompt * B] = jnp.dot(U2[...], M2[:, : prompt * B], preferred_element_type=F32)
    for t in range(prompt):
        S2[t] = (G1[t, 1].astype(F32) * conv_block(P2, t)).astype(BF16)
    back = {e: send(S2.at[(z + e) % nz], V.at[0, z], zpeer(e)) for e in far_first}
    fwd = [send(S2.at[z], V.at[1, z], sibling)]
    V[0, z] = S2[z]
    for sig, M_ref, P_ref, FS in ((signal, M1, P1, FS1), (U2[...], M2, P2, FS2)):
        P_ref[:, prompt * B :] = jnp.dot(sig, M_ref[:, prompt * B :], preferred_element_type=F32)
        for t in range(prompt, blocks):
            FS[t - prompt] = conv_block(P_ref, t)
    for copy in outw:
        copy.wait()
    for copy in wo_s:
        copy.wait_recv()
    for e in near_first:
        back[e].wait_recv()
        source = (z + nz - e) % nz
        fwd.append(send(V.at[0, source], V.at[1, source], sibling))
    for copy in fwd:
        copy.wait_recv()

    mixed = jnp.transpose(V[...].reshape(2 * B, B).astype(F32)).astype(BF16)

    def out_block(dy, dx):
        c = chip_of(dy, dx)
        weight = jnp.concatenate([Wc[c, 0], Wc[c, 1]], axis=0)
        block = jnp.dot(mixed, weight, preferred_element_type=F32)
        if dx == 0:
            OA[dy] = block[0:H]
        if dy == 0:
            OB[dx] = block[H:B]
        if dx or dy:
            PS[dy, dx] = block.astype(BF16)

    done = set()
    rs_a, rs_b = {}, {}
    for e in reversed(steps):
        s = slot_of[e]
        for d in range(q):
            for at in ((d, s), (s, d)):
                if at not in done:
                    done.add(at)
                    out_block(*at)
            if d == q - 1:
                rs_a[e] = send(PS.at[:, s, 0:H], RA.at[land(e)], xpeer(e))
                rs_b[e] = send(PS.at[s, :, H:B], RB.at[land(e)], ypeer(e))
    out_block(0, 0)

    future = []
    for FS, FL in ((FS1, FL1), (FS2, FL2)):
        future.append([send(FS.at[((z + e) % nz) // 2], FL.at[z], zpeer(e)) for e in far_first])
        FL[z] = FS[z // 2]

    def gather_sums(copies_in, O, R, Q):
        for copy in copies_in.values():
            copy.wait_recv()
        for d in range(q):
            total = O[d]
            for e in range(1, q):
                total += R[e, d].astype(F32)
            if d == 0:
                O[d] = total
            else:
                Q[d] = total.astype(BF16)

    gather_sums(rs_a, OA, RA, QA)
    rs_a2 = [send(QA.at[slot_of[e]], RA2.at[land(e)], ypeer(e)) for e in reversed(steps)]
    gather_sums(rs_b, OB, RB, QB)
    rs_b2 = [send(QB.at[slot_of[e]], RB2.at[land(e)], xpeer(e)) for e in reversed(steps)]

    for group, FL, ref in zip(future, (FL1, FL2), (ff, fs)):
        for copy in group:
            copy.wait_recv()
        rows = jnp.transpose(FL[...].reshape(B, B))
        ref[...] = jnp.where(z % 2 == 0, rows[0:H], rows[H:B])

    for group, O, R, rows in ((rs_a2, OA, RA2, slice(0, H)), (rs_b2, OB, RB2, slice(H, B))):
        for copy in group:
            copy.wait_recv()
        total = O[0]
        for e in range(1, q):
            total += R[e].astype(F32)
        out[rows, :] = total.astype(BF16)

    for copy in sent:
        copy.wait_send()
    assert counter[0] <= copies, counter[0]


def finish(a, b, c, out, ff, fs):
    out[...] = a[...]
    ff[...] = b[...]
    fs[...] = c[...]


def per_device(nz, tokens, input_weight, output_weight, filter_first, filter_second):
    depth, width = input_weight.shape[1:]
    chips = depth // (2 * B)
    q = int(round(chips**0.5))
    cz = B // nz
    taps = filter_first.shape[1]
    future = (taps // B - nz)
    copies = 160
    weights = input_weight.reshape(3, chips, 2, B, width)
    hbm = pl.BlockSpec(memory_space=pltpu.HBM)
    vmem = pl.BlockSpec(memory_space=pltpu.VMEM)
    scratch = [
        pltpu.VMEM((q, q, 2, B, B), BF16),
        pltpu.VMEM((chips, 2, B, 3 * B), BF16),
        pltpu.VMEM((chips, 2, B, B), BF16),
        pltpu.VMEM((B, 3 * B), F32),
        pltpu.VMEM((2, taps), BF16),
        pltpu.VMEM((2, taps), BF16),
        pltpu.VMEM((B, taps), BF16),
        pltpu.VMEM((B, taps), BF16),
        pltpu.VMEM((nz, cz, B), BF16),
        pltpu.VMEM((nz, 2, cz, B), BF16),
        pltpu.VMEM((nz, cz, B), BF16),
        pltpu.VMEM((nz, 2, cz, B), BF16),
        pltpu.VMEM((B, taps), F32),
        pltpu.VMEM((B, taps), F32),
        pltpu.VMEM((B, B), BF16),
        pltpu.VMEM((nz, cz, B), BF16),
        pltpu.VMEM((2, nz, cz, B), BF16),
        pltpu.VMEM((future, cz, B), F32),
        pltpu.VMEM((future, cz, B), F32),
        pltpu.VMEM((nz, cz, B), F32),
        pltpu.VMEM((nz, cz, B), F32),
        pltpu.VMEM((q, q, B, B), BF16),
        pltpu.VMEM((q, H, B), F32),
        pltpu.VMEM((q, H, B), F32),
        pltpu.VMEM((q, q, H, B), BF16),
        pltpu.VMEM((q, q, H, B), BF16),
        pltpu.VMEM((q, H, B), BF16),
        pltpu.VMEM((q, H, B), BF16),
        pltpu.VMEM((q, H, B), BF16),
        pltpu.VMEM((q, H, B), BF16),
        pltpu.SemaphoreType.DMA((copies,)),
        pltpu.SemaphoreType.DMA((copies,)),
        pltpu.SemaphoreType.DMA((9 + chips,)),
    ]
    operands = (tokens, weights, output_weight, filter_first, filter_second)
    operands = [pltpu.with_memory_space_constraint(a, pltpu.HBM) for a in operands]
    shapes = (
            jax.ShapeDtypeStruct((B, B), BF16),
            jax.ShapeDtypeStruct((H, B), F32),
            jax.ShapeDtypeStruct((H, B), F32),
        )
    parts = pl.pallas_call(
        functools.partial(kernel, q, nz, copies),
        out_shape=shapes,
        in_specs=[hbm] * 5,
        out_specs=(vmem, vmem, vmem),
        scratch_shapes=scratch,
        compiler_params=pltpu.CompilerParams(
            collective_id=0, has_side_effects=True, vmem_limit_bytes=32 * 2**20
        ),
    )(*operands)
    return pl.pallas_call(
        finish,
        out_shape=shapes,
        in_specs=[vmem] * 3,
        out_specs=(vmem, vmem, vmem),
        compiler_params=pltpu.CompilerParams(vmem_limit_bytes=2 * 2**20),
    )(*parts)


def solution(mesh):
    in_specs = (P("seq", "ch"), P(None, None, "ch"), P("ch", None), P("ch", None), P("ch", None))
    out_specs = (P("seq", "ch"), P("seq", "ch"), P("seq", "ch"))
    return jax.shard_map(
        functools.partial(per_device, mesh.shape["seq"]),
        mesh=mesh, in_specs=in_specs, out_specs=out_specs, check_vma=False,
    )
```

time: 50.5 us -> 44.4 us (0.88)
  local copies, waits for them, and re-layouts: 7.09 us -> 0 us
  Pallas kernels: 42.4 us -> 43.7 us
    unnamed x13 -> x0, local copies, waits for them, and re-layouts: 7.09 us -> none
    pallas_call x1 -> x2, Pallas kernels: 42.4 us -> 43.7 us  [the longest x1 43 us: per_device(): pl.pallas_call(functools.partial(kernel, q, nz, copies), out_shape=shapes...]
where the time goes in v2:
time: 44.4 us; the launch traced here: 44.3 us
  Pallas kernels  43.7 us (98%)
  between operations  0.64 us (1%)
    pallas_call x1, Pallas kernels, per_device(): pl.pallas_call(functools.partial(kernel, q, nz, copies), out_shape=shapes...  43 us

profile of v2, /device:TPU:1, one launch (start us, length us, event | category | flops | bytes accessed | tf_op | source)
XLA Modules:
  0.0 44.3 jit_solution(7612855509117761608)
XLA Ops:
  0.6 43.0 %shard_map.76 = (bf16[128,128]{1,0:T(8,128)(2,1)S(1)}, f32[64,128]{1,0:T(8,128)S(1)}, f32[64,128]{1,0:T(8,128)S(1)}) custom-call(bf16[128,128]{1,0:T(8,128)(2,1)} %tok.1, bf16[3,16,2,128,128]{4,3,2,1,0:T(8,128)(2,1)} %bitcast.1, bf16[128,4096]{1,0:T(8,128)(2,1)} %wo.1, bf16[2,1536]{1,0:T(2,128)(2,1)} %f1.1, bf16[2,1536]{1,0:T(2,128)(2,1)} %f2.1), custom_call_target="tpu_custom_call" | custom-call | tf_op jit(solution)/shard_map/pallas_call | solution.py:404
  43.7 0.6 %shard_map.77 = (bf16[128,128]{1,0:T(8,128)(2,1)}, f32[64,128]{1,0:T(8,128)}, f32[64,128]{1,0:T(8,128)}) custom-call(bf16[128,128]{1,0:T(8,128)(2,1)S(1)} %get-tuple-element.6.a, f32[64,128]{1,0:T(8,128)S(1)} %get-tuple-element.7.b, f32[64,128]{1,0:T(8,128)S(1)} %get-tuple-element.8.c), custom_call_target="tpu_custom_call" | custom-call | tf_op jit(solution)/shard_map/pallas_call | solution.py:414

commit v3 on v2

--- a/solution.py
+++ b/solution.py
@@ -32,9 +32,9 @@
     q, nz, copies,
     tok, wi, wo, f1, f2,
     out, ff, fs,
-    X, Wv, Wc, acc, F1v, F2v, M1, M2, S0, S1, G0, G1, P1, P2, U2, S2, V,
+    X, Wv, Wown, Wsib, acc, F1v, F2v, M1, M2, S0, S1, G0, G1, P1, P2, U2, S2, V,
     FS1, FS2, FL1, FL2, PS, OA, OB, RA, RB, QA, QB, RA2, RB2,
-    ssem, rsem, lsem,
+    ssem, rsem, lsem, plane_ready, column_ready,
 ):
     cz = B // nz
     prompt = nz
@@ -95,25 +95,34 @@
         return copy
 
     barrier = pltpu.get_barrier_semaphore()
-    partners = [zpeer(e) for e in far_first]
-    for e in range(1, q):
-        partners += [xpeer(e), ypeer(e)]
-    partners.append(sibling)
-    for device in partners:
+
+    def greet(device):
         pl.semaphore_signal(barrier, inc=1, device_id=device, device_id_type=MESH)
+
+    for e in steps:
+        greet((z, ch_of(y, (x + e) % q, 0)))
+        greet((z, ch_of((y + e) % q, x, 0)))
+
+    @pl.when(core == 1)
+    def _():
+        greet(sibling)
+
+    for e in far_first:
+        greet(((z + e) % nz, ch_of(y, x, 1)))
 
     own = local(tok, X.at[0, 0, 0])
     taps = [local(f1, F1v), local(f2, F2v)]
-    weights = []
-    for k, column in ((2, 0), (0, 1), (1, 2)):
-        for r in range(2):
-            weights.append(
-                local(
-                    wi.at[k, :, core if r == 0 else 1 - core],
-                    Wv.at[:, r, :, column * B : column * B + B],
-                )
-            )
-    pl.semaphore_wait(barrier, len(partners))
+    weights = [local(wi.at[k], Wv.at[part]) for part, k in enumerate((2, 0, 1))]
+
+    @pl.when(core == 0)
+    def _():
+        pl.semaphore_wait(barrier, 4 * (q - 1) + 1)
+        pl.semaphore_signal(plane_ready, inc=1, device_id=sibling, device_id_type=MESH)
+
+    @pl.when(core == 1)
+    def _():
+        pl.semaphore_wait(plane_ready, 1)
+
 
     ag_x, ag_y = {}, {}
     for e in steps:
@@ -154,9 +163,9 @@
         return ((y + offsets[dy]) % q) * q + (x + offsets[dx]) % q
 
     def terms(dy, dx, lo, hi):
-        tile = jnp.concatenate([X[dy, dx, 0], X[dy, dx, 1]], axis=1)
+        tile = jnp.concatenate([X[dy, dx, core], X[dy, dx, 1 - core]], axis=1)
         c = chip_of(dy, dx)
-        weight = jnp.concatenate([Wv[c, 0, :, lo:hi], Wv[c, 1, :, lo:hi]], axis=0)
+        weight = jnp.concatenate([Wv[part, c] for part in range(lo, hi)], axis=1)
         return jnp.dot(tile, weight, preferred_element_type=F32)
 
     def forward(g, e):
@@ -177,12 +186,12 @@
     for copy in weights:
         copy.wait()
     sib_own.wait_recv()
-    total = terms(0, 0, 0, 3 * B)
+    total = terms(0, 0, 0, 3)
     sib_x[0].wait_recv()
     sib_y[0].wait_recv()
     for d in early:
-        total += terms(0, d, 0, 3 * B)
-        total += terms(d, 0, 0, 3 * B)
+        total += terms(0, d, 0, 3)
+        total += terms(d, 0, 0, 3)
     acc[...] = total
     first_fwd = []
     for e in near_e:
@@ -191,50 +200,51 @@
     for g, es in [(0, far_e)] + [(g, near_e + far_e) for g in range(1, len(groups))]:
         for e in es:
             last_fwd += forward(g, e)
+
+    @pl.when(core == 1)
+    def _():
+        pl.semaphore_wait(barrier, 2 * (nz - 1))
+        pl.semaphore_signal(column_ready, inc=1, device_id=sibling, device_id_type=MESH)
+
     total = acc[...]
     for g in range(1, len(groups)):
         sib_x[g].wait_recv()
         sib_y[g].wait_recv()
         for d in range(*groups[g]):
-            total += terms(0, d, 0, 3 * B)
-            total += terms(d, 0, 0, 3 * B)
+            total += terms(0, d, 0, 3)
+            total += terms(d, 0, 0, 3)
     for copy in first_fwd:
         copy.wait_recv()
     for dy in early:
         for dx in early:
-            total += terms(dy, dx, 0, 3 * B)
+            total += terms(dy, dx, 0, 3)
     acc[...] = total
     for copy in last_fwd:
         copy.wait_recv()
+
+    @pl.when(core == 0)
+    def _():
+        pl.semaphore_wait(column_ready, 1)
+
 
     rest = [(dy, dx) for dy in range(1, q) for dx in range(1, q) if dy in late or dx in late]
     total = acc[:, 0:B]
     for dy, dx in rest:
-        total += terms(dy, dx, 0, B)
+        total += terms(dy, dx, 0, 1)
     S0[...] = jnp.transpose(total).astype(BF16).reshape(nz, cz, B)
     a2a_value = [send(S0.at[(z + e) % nz], G0.at[z], zpeer(e)) for e in far_first]
     G0[z] = S0[z]
     total = acc[:, B : 3 * B]
     for dy, dx in rest:
-        total += terms(dy, dx, B, 3 * B)
+        total += terms(dy, dx, 1, 3)
     for part in range(2):
         flipped = jnp.transpose(total[:, part * B : part * B + B])
         S1[:, part] = flipped.astype(BF16).reshape(nz, cz, B)
     a2a_gates = [send(S1.at[(z + e) % nz], G1.at[z], zpeer(e)) for e in far_first]
     G1[z] = S1[z]
 
-    outw, wo_s = [], []
-    for c in range(q * q):
-        outw.append(
-            local(wo.at[:, pl.ds(pl.multiple_of((2 * c + core) * B, B), B)], Wc.at[c, 0])
-        )
-        wo_s.append(
-            send(
-                wo.at[:, pl.ds(pl.multiple_of((2 * c + 1 - core) * B, B), B)],
-                Wc.at[c, 1],
-                sibling,
-            )
-        )
+    outw = [local(wo, Wown)]
+    wo_s = [send(wo, Wsib, sibling)]
 
     def conv_block(P_ref, t):
         total = None
@@ -278,7 +288,8 @@
 
     def out_block(dy, dx):
         c = chip_of(dy, dx)
-        weight = jnp.concatenate([Wc[c, 0], Wc[c, 1]], axis=0)
+        columns = pl.ds(pl.multiple_of((2 * c + core) * B, B), B)
+        weight = jnp.concatenate([Wown[:, columns], Wsib[:, columns]], axis=0)
         block = jnp.dot(mixed, weight, preferred_element_type=F32)
         if dx == 0:
             OA[dy] = block[0:H]
@@ -356,13 +367,14 @@
     taps = filter_first.shape[1]
     future = (taps // B - nz)
     copies = 160
-    weights = input_weight.reshape(3, chips, 2, B, width)
+    weights = input_weight.reshape(3, chips, 2 * B, width)
     hbm = pl.BlockSpec(memory_space=pltpu.HBM)
     vmem = pl.BlockSpec(memory_space=pltpu.VMEM)
     scratch = [
         pltpu.VMEM((q, q, 2, B, B), BF16),
-        pltpu.VMEM((chips, 2, B, 3 * B), BF16),
-        pltpu.VMEM((chips, 2, B, B), BF16),
+        pltpu.VMEM((3, chips, 2 * B, B), BF16),
+        pltpu.VMEM((B, 2 * chips * B), BF16),
+        pltpu.VMEM((B, 2 * chips * B), BF16),
         pltpu.VMEM((B, 3 * B), F32),
         pltpu.VMEM((2, taps), BF16),
         pltpu.VMEM((2, taps), BF16),
@@ -392,7 +404,9 @@
         pltpu.VMEM((q, H, B), BF16),
         pltpu.SemaphoreType.DMA((copies,)),
         pltpu.SemaphoreType.DMA((copies,)),
-        pltpu.SemaphoreType.DMA((9 + chips,)),
+        pltpu.SemaphoreType.DMA((8,)),
+        pltpu.SemaphoreType.REGULAR,
+        pltpu.SemaphoreType.REGULAR,
     ]
     operands = (tokens, weights, output_weight, filter_first, filter_second)
     operands = [pltpu.with_memory_space_constraint(a, pltpu.HBM) for a in operands]

time: 44.4 us -> 42.1 us (0.948)
  Pallas kernels: 43.7 us -> 41.4 us
    pallas_call x1, Pallas kernels: 43 us -> 40.7 us  [per_device(): pl.pallas_call(functools.partial(kernel, q, nz, copies), out_shape=shapes...]
where the time goes in v3:
time: 42.1 us; the launch traced here: 42 us
  Pallas kernels  41.4 us (98%)
  between operations  0.64 us (2%)
    pallas_call x1, Pallas kernels, per_device(): pl.pallas_call(functools.partial(kernel, q, nz, copies), out_shape=shapes...  40.7 us

profile of v3, /device:TPU:1, one launch (start us, length us, event | category | flops | bytes accessed | tf_op | source)
XLA Modules:
  0.0 42.0 jit_solution(14929674767956955788)
XLA Ops:
  0.6 40.7 %shard_map.76 = (bf16[128,128]{1,0:T(8,128)(2,1)S(1)}, f32[64,128]{1,0:T(8,128)S(1)}, f32[64,128]{1,0:T(8,128)S(1)}) custom-call(bf16[128,128]{1,0:T(8,128)(2,1)} %tok.1, bf16[3,16,256,128]{3,2,1,0:T(8,128)(2,1)} %bitcast.1, bf16[128,4096]{1,0:T(8,128)(2,1)} %wo.1, bf16[2,1536]{1,0:T(2,128)(2,1)} %f1.1, bf16[2,1536]{1,0:T(2,128)(2,1)} %f2.1), custom_call_target="tpu_custom_call" | custom-call | tf_op jit(solution)/shard_map/pallas_call | solution.py:418
  41.4 0.6 %shard_map.77 = (bf16[128,128]{1,0:T(8,128)(2,1)}, f32[64,128]{1,0:T(8,128)}, f32[64,128]{1,0:T(8,128)}) custom-call(bf16[128,128]{1,0:T(8,128)(2,1)S(1)} %get-tuple-element.6.a, f32[64,128]{1,0:T(8,128)S(1)} %get-tuple-element.7.b, f32[64,128]{1,0:T(8,128)S(1)} %get-tuple-element.8.c), custom_call_target="tpu_custom_call" | custom-call | tf_op jit(solution)/shard_map/pallas_call | solution.py:428

commit v4 on v3

--- a/solution.py
+++ b/solution.py
@@ -32,7 +32,7 @@
     q, nz, copies,
     tok, wi, wo, f1, f2,
     out, ff, fs,
-    X, Wv, Wown, Wsib, acc, F1v, F2v, M1, M2, S0, S1, G0, G1, P1, P2, U2, S2, V,
+    X, Wv, Wown, Wsib, acc, F, M1, M2, S0, S1, G0, G1, P1, P2, U2, S2, V,
     FS1, FS2, FL1, FL2, PS, OA, OB, RA, RB, QA, QB, RA2, RB2,
     ssem, rsem, lsem, plane_ready, column_ready,
 ):
@@ -71,28 +71,31 @@
     far_first = sorted(range(1, nz), key=lambda e: -min(e, nz - e))
     near_first = sorted(range(1, nz), key=lambda e: min(e, nz - e))
 
-    counter = [0]
+    counts = {"send": 0, "receive": 0}
     sent = []
 
-    def send(src, dst, device):
-        i = counter[0]
-        counter[0] += 1
-        copy = pltpu.make_async_remote_copy(
-            src_ref=src, dst_ref=dst, send_sem=ssem.at[i], recv_sem=rsem.at[i],
+    def fresh(kind):
+        counts[kind] += 1
+        return counts[kind] - 1
+
+    def transfer(src, dst, device, s, r):
+        return pltpu.make_async_remote_copy(
+            src_ref=src, dst_ref=dst, send_sem=ssem.at[s], recv_sem=rsem.at[r],
             device_id=device, device_id_type=MESH,
         )
-        copy.start()
-        sent.append(copy)
-        return copy
-
-    local_count = [0]
-
-    def local(src, dst):
-        i = local_count[0]
-        local_count[0] += 1
-        copy = pltpu.make_async_copy(src, dst, lsem.at[i])
+
+    def out_of(ref):
+        s = fresh("send")
+        sent.append((ref, s))
+        return s
+
+    def send(src, dst, device, s, r):
+        copy = transfer(src, dst, device, s, r)
         copy.start()
         return copy
+
+    def landed(ref, r):
+        transfer(ref, ref, sibling, 0, r).wait_recv()
 
     barrier = pltpu.get_barrier_semaphore()
 
@@ -110,9 +113,13 @@
     for e in far_first:
         greet(((z + e) % nz, ch_of(y, x, 1)))
 
-    own = local(tok, X.at[0, 0, 0])
-    taps = [local(f1, F1v), local(f2, F2v)]
-    weights = [local(wi.at[k], Wv.at[part]) for part, k in enumerate((2, 0, 1))]
+    own = pltpu.make_async_copy(tok, X.at[0, 0, 0], lsem.at[0])
+    own.start()
+    for i, ref in enumerate((f1, f2)):
+        pltpu.make_async_copy(ref, F.at[i], lsem.at[1]).start()
+    for part, k in enumerate((2, 0, 1)):
+        pltpu.make_async_copy(wi.at[k], Wv.at[part], lsem.at[2]).start()
+    own.wait()
 
     @pl.when(core == 0)
     def _():
@@ -124,40 +131,53 @@
         pl.semaphore_wait(plane_ready, 1)
 
 
-    ag_x, ag_y = {}, {}
+    s = out_of(X.at[0, 0 : q - 1])
+    ag_x = [fresh("receive") for _ in groups]
+    ag_y = [fresh("receive") for _ in groups]
+
+    def group_of(slot):
+        return [lo <= slot < hi for lo, hi in groups].index(True)
+
     for e in steps:
-        ag_x[e] = send(tok, X.at[0, land(e), 0], xpeer(e))
-        ag_y[e] = send(tok, X.at[land(e), 0, 0], ypeer(e))
-    sib_own = send(tok, X.at[0, 0, 1], sibling)
+        g = group_of(land(e))
+        send(X.at[0, 0, 0], X.at[0, land(e), 0], xpeer(e), s, ag_x[g])
+        send(X.at[0, 0, 0], X.at[land(e), 0, 0], ypeer(e), s, ag_y[g])
+    sib_own = send(
+        X.at[0, 0, 0], X.at[0, 0, 1], sibling, out_of(X.at[0, 0, 0]), fresh("receive")
+    )
 
     first_head = z * cz < H
 
-    def head_taps(ref):
-        both = ref[...].astype(F32)
+    def head_taps(i):
+        both = F[i].astype(F32)
         return jnp.where(first_head, both[0:1], both[1:2])
 
-    for copy in taps:
-        copy.wait()
-    build_toeplitz(head_taps(F1v), M1)
-
-    sib_x, sib_y, ag_a, ag_b = [], [], [], []
+    pltpu.make_async_copy(F, F, lsem.at[1]).wait()
+    build_toeplitz(head_taps(0), M1)
+
+    sib_xy, ag_a, ag_b = [], [], []
     for g, (lo, hi) in enumerate(groups):
-        for e in range(1, q):
-            if lo <= land(e) < hi:
-                ag_x[e].wait_recv()
-        ag_a.append(
-            {e: send(X.at[0, lo:hi, 0, 0:H], X.at[land(e), lo:hi, 0, 0:H], ypeer(e)) for e in steps}
-        )
-        for e in range(1, q):
-            if lo <= land(e) < hi:
-                ag_y[e].wait_recv()
-        ag_b.append(
-            {e: send(X.at[lo:hi, 0, 0, H:B], X.at[lo:hi, land(e), 0, H:B], xpeer(e)) for e in steps}
-        )
-        sib_x.append(send(X.at[0, lo:hi, 0], X.at[0, lo:hi, 1], sibling))
-        sib_y.append(send(X.at[lo:hi, 0, 0], X.at[lo:hi, 0, 1], sibling))
+        s = out_of(X.at[0 : hi - lo, 0 : q - 1, 0])
+        landed(X.at[0, lo:hi, 0], ag_x[g])
+        ag_a.append({
+            e: send(
+                X.at[0, lo:hi, 0, 0:H], X.at[land(e), lo:hi, 0, 0:H], ypeer(e), s, fresh("receive")
+            )
+            for e in steps
+        })
+        landed(X.at[lo:hi, 0, 0], ag_y[g])
+        ag_b.append({
+            e: send(
+                X.at[lo:hi, 0, 0, H:B], X.at[lo:hi, land(e), 0, H:B], xpeer(e), s, fresh("receive")
+            )
+            for e in steps
+        })
+        s, r = out_of(X.at[0, lo:hi]), fresh("receive")
+        send(X.at[0, lo:hi, 0], X.at[0, lo:hi, 1], sibling, s, r)
+        send(X.at[lo:hi, 0, 0], X.at[lo:hi, 0, 1], sibling, s, r)
+        sib_xy.append(r)
         if g == 0:
-            build_toeplitz(head_taps(F2v), M2)
+            build_toeplitz(head_taps(1), M2)
 
     def chip_of(dy, dx):
         return ((y + offsets[dy]) % q) * q + (x + offsets[dx]) % q
@@ -168,38 +188,45 @@
         weight = jnp.concatenate([Wv[part, c] for part in range(lo, hi)], axis=1)
         return jnp.dot(tile, weight, preferred_element_type=F32)
 
-    def forward(g, e):
+    def forward(g, e, s, r):
         lo, hi = groups[g]
-        s = land(e)
+        at = land(e)
         ag_a[g][e].wait_recv()
-        a = send(X.at[s, lo:hi, 0, 0:H], X.at[s, lo:hi, 1, 0:H], sibling)
+        send(X.at[at, lo:hi, 0, 0:H], X.at[at, lo:hi, 1, 0:H], sibling, s, r)
         ag_b[g][e].wait_recv()
-        b = send(X.at[lo:hi, s, 0, H:B], X.at[lo:hi, s, 1, H:B], sibling)
-        return [a, b]
+        send(X.at[lo:hi, at, 0, H:B], X.at[lo:hi, at, 1, H:B], sibling, s, r)
 
     early = list(range(1, 1 + len(near)))
     late = list(range(1 + len(near), q))
     near_e = [e for e in range(1, q) if land(e) in early]
     far_e = [e for e in range(1, q) if land(e) in late]
 
-    own.wait()
-    for copy in weights:
-        copy.wait()
+    pltpu.make_async_copy(Wv, Wv, lsem.at[2]).wait()
     sib_own.wait_recv()
     total = terms(0, 0, 0, 3)
-    sib_x[0].wait_recv()
-    sib_y[0].wait_recv()
+    landed(X.at[0, 1 : 1 + len(near)], sib_xy[0])
     for d in early:
         total += terms(0, d, 0, 3)
         total += terms(d, 0, 0, 3)
     acc[...] = total
-    first_fwd = []
+    corner = X.at[1 : 1 + len(near), 1 : 1 + len(near), 1]
+    s, first_fwd = out_of(corner), fresh("receive")
     for e in near_e:
-        first_fwd += forward(0, e)
+        forward(0, e, s, first_fwd)
     last_fwd = []
-    for g, es in [(0, far_e)] + [(g, near_e + far_e) for g in range(1, len(groups))]:
-        for e in es:
-            last_fwd += forward(g, e)
+    if far_e:
+        ref = X.at[1 + len(near) : q, 1 : 1 + len(near), 1]
+        s, r = out_of(ref), fresh("receive")
+        last_fwd.append((ref, r))
+        for e in far_e:
+            forward(0, e, s, r)
+    for g in range(1, len(groups)):
+        lo, hi = groups[g]
+        ref = X.at[lo:hi, 1:q, 1]
+        s, r = out_of(ref), fresh("receive")
+        last_fwd.append((ref, r))
+        for e in near_e + far_e:
+            forward(g, e, s, r)
 
     @pl.when(core == 1)
     def _():
@@ -208,19 +235,17 @@
 
     total = acc[...]
     for g in range(1, len(groups)):
-        sib_x[g].wait_recv()
-        sib_y[g].wait_recv()
+        landed(X.at[0, groups[g][0] : groups[g][1]], sib_xy[g])
         for d in range(*groups[g]):
             total += terms(0, d, 0, 3)
             total += terms(d, 0, 0, 3)
-    for copy in first_fwd:
-        copy.wait_recv()
+    landed(corner, first_fwd)
     for dy in early:
         for dx in early:
             total += terms(dy, dx, 0, 3)
     acc[...] = total
-    for copy in last_fwd:
-        copy.wait_recv()
+    for ref, r in last_fwd:
+        landed(ref, r)
 
     @pl.when(core == 0)
     def _():
@@ -232,7 +257,9 @@
     for dy, dx in rest:
         total += terms(dy, dx, 0, 1)
     S0[...] = jnp.transpose(total).astype(BF16).reshape(nz, cz, B)
-    a2a_value = [send(S0.at[(z + e) % nz], G0.at[z], zpeer(e)) for e in far_first]
+    s, value_in = out_of(S0.at[0 : nz - 1]), fresh("receive")
+    for e in far_first:
+        send(S0.at[(z + e) % nz], G0.at[z], zpeer(e), s, value_in)
     G0[z] = S0[z]
     total = acc[:, B : 3 * B]
     for dy, dx in rest:
@@ -240,11 +267,14 @@
     for part in range(2):
         flipped = jnp.transpose(total[:, part * B : part * B + B])
         S1[:, part] = flipped.astype(BF16).reshape(nz, cz, B)
-    a2a_gates = [send(S1.at[(z + e) % nz], G1.at[z], zpeer(e)) for e in far_first]
+    s, gates_in = out_of(S1.at[0 : nz - 1]), fresh("receive")
+    for e in far_first:
+        send(S1.at[(z + e) % nz], G1.at[z], zpeer(e), s, gates_in)
     G1[z] = S1[z]
 
-    outw = [local(wo, Wown)]
-    wo_s = [send(wo, Wsib, sibling)]
+    own_rows = pltpu.make_async_copy(wo, Wown, lsem.at[3])
+    own_rows.start()
+    sibling_rows = send(wo, Wsib, sibling, out_of(Wsib), fresh("receive"))
 
     def conv_block(P_ref, t):
         total = None
@@ -254,35 +284,34 @@
                 total = term if total is None else total + term
         return total
 
-    for copy in a2a_value:
-        copy.wait_recv()
+    landed(G0.at[0 : nz - 1], value_in)
     signal = G0[...].reshape(B, B)
     P1[:, : prompt * B] = jnp.dot(signal, M1[:, : prompt * B], preferred_element_type=F32)
-    for copy in a2a_gates:
-        copy.wait_recv()
+    landed(G1.at[0 : nz - 1], gates_in)
     for t in range(prompt):
         mixed = (G1[t, 0].astype(F32) * conv_block(P1, t)).astype(BF16)
         U2[t * cz : t * cz + cz, :] = mixed
     P2[:, : prompt * B] = jnp.dot(U2[...], M2[:, : prompt * B], preferred_element_type=F32)
     for t in range(prompt):
         S2[t] = (G1[t, 1].astype(F32) * conv_block(P2, t)).astype(BF16)
-    back = {e: send(S2.at[(z + e) % nz], V.at[0, z], zpeer(e)) for e in far_first}
-    fwd = [send(S2.at[z], V.at[1, z], sibling)]
+    s = out_of(S2.at[0 : nz - 1])
+    back = {
+        e: send(S2.at[(z + e) % nz], V.at[0, z], zpeer(e), s, fresh("receive")) for e in far_first
+    }
+    s, fwd = out_of(V.at[1]), fresh("receive")
+    send(S2.at[z], V.at[1, z], sibling, s, fwd)
     V[0, z] = S2[z]
     for sig, M_ref, P_ref, FS in ((signal, M1, P1, FS1), (U2[...], M2, P2, FS2)):
         P_ref[:, prompt * B :] = jnp.dot(sig, M_ref[:, prompt * B :], preferred_element_type=F32)
         for t in range(prompt, blocks):
             FS[t - prompt] = conv_block(P_ref, t)
-    for copy in outw:
-        copy.wait()
-    for copy in wo_s:
-        copy.wait_recv()
+    own_rows.wait()
+    sibling_rows.wait_recv()
     for e in near_first:
         back[e].wait_recv()
         source = (z + nz - e) % nz
-        fwd.append(send(V.at[0, source], V.at[1, source], sibling))
-    for copy in fwd:
-        copy.wait_recv()
+        send(V.at[0, source], V.at[1, source], sibling, s, fwd)
+    landed(V.at[1], fwd)
 
     mixed = jnp.transpose(V[...].reshape(2 * B, B).astype(F32)).astype(BF16)
 
@@ -299,7 +328,7 @@
             PS[dy, dx] = block.astype(BF16)
 
     done = set()
-    rs_a, rs_b = {}, {}
+    (sa, rs_a), (sb, rs_b) = ((out_of(R.at[1:q]), fresh("receive")) for R in (RA, RB))
     for e in reversed(steps):
         s = slot_of[e]
         for d in range(q):
@@ -308,18 +337,20 @@
                     done.add(at)
                     out_block(*at)
             if d == q - 1:
-                rs_a[e] = send(PS.at[:, s, 0:H], RA.at[land(e)], xpeer(e))
-                rs_b[e] = send(PS.at[s, :, H:B], RB.at[land(e)], ypeer(e))
+                send(PS.at[:, s, 0:H], RA.at[land(e)], xpeer(e), sa, rs_a)
+                send(PS.at[s, :, H:B], RB.at[land(e)], ypeer(e), sb, rs_b)
     out_block(0, 0)
 
     future = []
     for FS, FL in ((FS1, FL1), (FS2, FL2)):
-        future.append([send(FS.at[((z + e) % nz) // 2], FL.at[z], zpeer(e)) for e in far_first])
+        s, r = out_of(FL.at[0 : nz - 1]), fresh("receive")
+        for e in far_first:
+            send(FS.at[((z + e) % nz) // 2], FL.at[z], zpeer(e), s, r)
+        future.append(r)
         FL[z] = FS[z // 2]
 
-    def gather_sums(copies_in, O, R, Q):
-        for copy in copies_in.values():
-            copy.wait_recv()
+    def gather_sums(r, O, R, Q):
+        landed(R.at[1:q], r)
         for d in range(q):
             total = O[d]
             for e in range(1, q):
@@ -330,27 +361,29 @@
                 Q[d] = total.astype(BF16)
 
     gather_sums(rs_a, OA, RA, QA)
-    rs_a2 = [send(QA.at[slot_of[e]], RA2.at[land(e)], ypeer(e)) for e in reversed(steps)]
+    s, rs_a2 = out_of(RA2.at[1:q]), fresh("receive")
+    for e in reversed(steps):
+        send(QA.at[slot_of[e]], RA2.at[land(e)], ypeer(e), s, rs_a2)
     gather_sums(rs_b, OB, RB, QB)
-    rs_b2 = [send(QB.at[slot_of[e]], RB2.at[land(e)], xpeer(e)) for e in reversed(steps)]
-
-    for group, FL, ref in zip(future, (FL1, FL2), (ff, fs)):
-        for copy in group:
-            copy.wait_recv()
+    s, rs_b2 = out_of(RB2.at[1:q]), fresh("receive")
+    for e in reversed(steps):
+        send(QB.at[slot_of[e]], RB2.at[land(e)], xpeer(e), s, rs_b2)
+
+    for r, FL, ref in zip(future, (FL1, FL2), (ff, fs)):
+        landed(FL.at[0 : nz - 1], r)
         rows = jnp.transpose(FL[...].reshape(B, B))
         ref[...] = jnp.where(z % 2 == 0, rows[0:H], rows[H:B])
 
-    for group, O, R, rows in ((rs_a2, OA, RA2, slice(0, H)), (rs_b2, OB, RB2, slice(H, B))):
-        for copy in group:
-            copy.wait_recv()
+    for r, O, R, rows in ((rs_a2, OA, RA2, slice(0, H)), (rs_b2, OB, RB2, slice(H, B))):
+        landed(R.at[1:q], r)
         total = O[0]
         for e in range(1, q):
             total += R[e].astype(F32)
         out[rows, :] = total.astype(BF16)
 
-    for copy in sent:
-        copy.wait_send()
-    assert counter[0] <= copies, counter[0]
+    for ref, s in sent:
+        transfer(ref, ref, sibling, s, 0).wait_send()
+    assert counts == {"send": copies[0], "receive": copies[1]}, counts
 
 
 def finish(a, b, c, out, ff, fs):
@@ -366,7 +399,11 @@
     cz = B // nz
     taps = filter_first.shape[1]
     future = (taps // B - nz)
-    copies = 160
+    groups = 2 if q > 2 else 1
+    copies = (
+        1 + 1 + 2 * groups + 1 + (2 * groups - 2) + 11,
+        2 * groups + 1 + 2 * groups * (q - 1) + groups + 1 + (2 * groups - 2) + 3 + nz + 6,
+    )
     weights = input_weight.reshape(3, chips, 2 * B, width)
     hbm = pl.BlockSpec(memory_space=pltpu.HBM)
     vmem = pl.BlockSpec(memory_space=pltpu.VMEM)
@@ -376,8 +413,7 @@
         pltpu.VMEM((B, 2 * chips * B), BF16),
         pltpu.VMEM((B, 2 * chips * B), BF16),
         pltpu.VMEM((B, 3 * B), F32),
-        pltpu.VMEM((2, taps), BF16),
-        pltpu.VMEM((2, taps), BF16),
+        pltpu.VMEM((2, 2, taps), BF16),
         pltpu.VMEM((B, taps), BF16),
         pltpu.VMEM((B, taps), BF16),
         pltpu.VMEM((nz, cz, B), BF16),
@@ -402,9 +438,9 @@
         pltpu.VMEM((q, H, B), BF16),
         pltpu.VMEM((q, H, B), BF16),
         pltpu.VMEM((q, H, B), BF16),
-        pltpu.SemaphoreType.DMA((copies,)),
-        pltpu.SemaphoreType.DMA((copies,)),
-        pltpu.SemaphoreType.DMA((8,)),
+        pltpu.SemaphoreType.DMA((copies[0],)),
+        pltpu.SemaphoreType.DMA((copies[1],)),
+        pltpu.SemaphoreType.DMA((4,)),
         pltpu.SemaphoreType.REGULAR,
         pltpu.SemaphoreType.REGULAR,
     ]

time: 42.1 us -> 39.3 us (0.933)
  Pallas kernels: 41.4 us -> 38.6 us
    pallas_call x1, Pallas kernels: 40.7 us -> 38 us  [per_device(): pl.pallas_call(functools.partial(kernel, q, nz, copies), out_shape=shapes...]
where the time goes in v4:
time: 39.3 us
  Pallas kernels  38.6 us (98%)
  between operations  0.64 us (2%)
    pallas_call x1, Pallas kernels, per_device(): pl.pallas_call(functools.partial(kernel, q, nz, copies), out_shape=shapes...  38 us

profile of v4, /device:TPU:1, one launch (start us, length us, event | category | flops | bytes accessed | tf_op | source)
XLA Modules:
  0.0 39.3 jit_solution(1559977593598926643)
XLA Ops:
  0.6 38.0 %shard_map.76 = (bf16[128,128]{1,0:T(8,128)(2,1)S(1)}, f32[64,128]{1,0:T(8,128)S(1)}, f32[64,128]{1,0:T(8,128)S(1)}) custom-call(bf16[128,128]{1,0:T(8,128)(2,1)} %tok.1, bf16[3,16,256,128]{3,2,1,0:T(8,128)(2,1)} %bitcast.1, bf16[128,4096]{1,0:T(8,128)(2,1)} %wo.1, bf16[2,1536]{1,0:T(2,128)(2,1)} %f1.1, bf16[2,1536]{1,0:T(2,128)(2,1)} %f2.1), custom_call_target="tpu_custom_call" | custom-call | tf_op jit(solution)/shard_map/pallas_call | solution.py:454
  38.6 0.6 %shard_map.77 = (bf16[128,128]{1,0:T(8,128)(2,1)}, f32[64,128]{1,0:T(8,128)}, f32[64,128]{1,0:T(8,128)}) custom-call(bf16[128,128]{1,0:T(8,128)(2,1)S(1)} %get-tuple-element.6.a, f32[64,128]{1,0:T(8,128)S(1)} %get-tuple-element.7.b, f32[64,128]{1,0:T(8,128)S(1)} %get-tuple-element.8.c), custom_call_target="tpu_custom_call" | custom-call | tf_op jit(solution)/shard_map/pallas_call | solution.py:464

commit v5 on v4

--- a/solution.py
+++ b/solution.py
@@ -261,16 +261,17 @@
     for e in far_first:
         send(S0.at[(z + e) % nz], G0.at[z], zpeer(e), s, value_in)
     G0[z] = S0[z]
-    total = acc[:, B : 3 * B]
-    for dy, dx in rest:
-        total += terms(dy, dx, 1, 3)
+    gates_in = []
     for part in range(2):
-        flipped = jnp.transpose(total[:, part * B : part * B + B])
-        S1[:, part] = flipped.astype(BF16).reshape(nz, cz, B)
-    s, gates_in = out_of(S1.at[0 : nz - 1]), fresh("receive")
-    for e in far_first:
-        send(S1.at[(z + e) % nz], G1.at[z], zpeer(e), s, gates_in)
-    G1[z] = S1[z]
+        total = acc[:, part * B + B : part * B + 2 * B]
+        for dy, dx in rest:
+            total += terms(dy, dx, part + 1, part + 2)
+        S1[part] = jnp.transpose(total).astype(BF16).reshape(nz, cz, B)
+        s, r = out_of(S1.at[part, 0 : nz - 1]), fresh("receive")
+        for e in far_first:
+            send(S1.at[part, (z + e) % nz], G1.at[part, z], zpeer(e), s, r)
+        G1[part, z] = S1[part, z]
+        gates_in.append(r)
 
     own_rows = pltpu.make_async_copy(wo, Wown, lsem.at[3])
     own_rows.start()
@@ -287,13 +288,14 @@
     landed(G0.at[0 : nz - 1], value_in)
     signal = G0[...].reshape(B, B)
     P1[:, : prompt * B] = jnp.dot(signal, M1[:, : prompt * B], preferred_element_type=F32)
-    landed(G1.at[0 : nz - 1], gates_in)
+    landed(G1.at[0, 0 : nz - 1], gates_in[0])
     for t in range(prompt):
-        mixed = (G1[t, 0].astype(F32) * conv_block(P1, t)).astype(BF16)
+        mixed = (G1[0, t].astype(F32) * conv_block(P1, t)).astype(BF16)
         U2[t * cz : t * cz + cz, :] = mixed
     P2[:, : prompt * B] = jnp.dot(U2[...], M2[:, : prompt * B], preferred_element_type=F32)
+    landed(G1.at[1, 0 : nz - 1], gates_in[1])
     for t in range(prompt):
-        S2[t] = (G1[t, 1].astype(F32) * conv_block(P2, t)).astype(BF16)
+        S2[t] = (G1[1, t].astype(F32) * conv_block(P2, t)).astype(BF16)
     s = out_of(S2.at[0 : nz - 1])
     back = {
         e: send(S2.at[(z + e) % nz], V.at[0, z], zpeer(e), s, fresh("receive")) for e in far_first
@@ -311,9 +313,11 @@
         back[e].wait_recv()
         source = (z + nz - e) % nz
         send(V.at[0, source], V.at[1, source], sibling, s, fwd)
+    own_half = jnp.transpose(V[0].reshape(B, B).astype(F32)).astype(BF16)
     landed(V.at[1], fwd)
 
-    mixed = jnp.transpose(V[...].reshape(2 * B, B).astype(F32)).astype(BF16)
+    other_half = jnp.transpose(V[1].reshape(B, B).astype(F32)).astype(BF16)
+    mixed = jnp.concatenate([own_half, other_half], axis=1)
 
     def out_block(dy, dx):
         c = chip_of(dy, dx)
@@ -401,8 +405,8 @@
     future = (taps // B - nz)
     groups = 2 if q > 2 else 1
     copies = (
-        1 + 1 + 2 * groups + 1 + (2 * groups - 2) + 11,
-        2 * groups + 1 + 2 * groups * (q - 1) + groups + 1 + (2 * groups - 2) + 3 + nz + 6,
+        1 + 1 + 2 * groups + 1 + (2 * groups - 2) + 12,
+        2 * groups + 1 + 2 * groups * (q - 1) + groups + 1 + (2 * groups - 2) + 4 + nz + 6,
     )
     weights = input_weight.reshape(3, chips, 2 * B, width)
     hbm = pl.BlockSpec(memory_space=pltpu.HBM)
@@ -417,9 +421,9 @@
         pltpu.VMEM((B, taps), BF16),
         pltpu.VMEM((B, taps), BF16),
         pltpu.VMEM((nz, cz, B), BF16),
-        pltpu.VMEM((nz, 2, cz, B), BF16),
+        pltpu.VMEM((2, nz, cz, B), BF16),
         pltpu.VMEM((nz, cz, B), BF16),
-        pltpu.VMEM((nz, 2, cz, B), BF16),
+        pltpu.VMEM((2, nz, cz, B), BF16),
         pltpu.VMEM((B, taps), F32),
         pltpu.VMEM((B, taps), F32),
         pltpu.VMEM((B, B), BF16),

time: 39.3 us -> 39.2 us (level)
  no operation moved by 1% of the time
where the time goes in v5:
time: 39.2 us; the launch traced here: 39.1 us
  Pallas kernels  38.5 us (98%)
  between operations  0.64 us (2%)
    pallas_call x1, Pallas kernels, per_device(): pl.pallas_call(functools.partial(kernel, q, nz, copies), out_shape=shapes...  37.9 us

profile of v5, /device:TPU:1, one launch (start us, length us, event | category | flops | bytes accessed | tf_op | source)
XLA Modules:
  0.0 39.1 jit_solution(4866579539725159318)
XLA Ops:
  0.6 37.9 %shard_map.76 = (bf16[128,128]{1,0:T(8,128)(2,1)S(1)}, f32[64,128]{1,0:T(8,128)S(1)}, f32[64,128]{1,0:T(8,128)S(1)}) custom-call(bf16[128,128]{1,0:T(8,128)(2,1)} %tok.1, bf16[3,16,256,128]{3,2,1,0:T(8,128)(2,1)} %bitcast.1, bf16[128,4096]{1,0:T(8,128)(2,1)} %wo.1, bf16[2,1536]{1,0:T(2,128)(2,1)} %f1.1, bf16[2,1536]{1,0:T(2,128)(2,1)} %f2.1), custom_call_target="tpu_custom_call" | custom-call | tf_op jit(solution)/shard_map/pallas_call | solution.py:458
  38.5 0.6 %shard_map.77 = (bf16[128,128]{1,0:T(8,128)(2,1)}, f32[64,128]{1,0:T(8,128)}, f32[64,128]{1,0:T(8,128)}) custom-call(bf16[128,128]{1,0:T(8,128)(2,1)S(1)} %get-tuple-element.6.a, f32[64,128]{1,0:T(8,128)S(1)} %get-tuple-element.7.b, f32[64,128]{1,0:T(8,128)S(1)} %get-tuple-element.8.c), custom_call_target="tpu_custom_call" | custom-call | tf_op jit(solution)/shard_map/pallas_call | solution.py:468

commit v6 on v5

--- a/solution.py
+++ b/solution.py
@@ -97,6 +97,8 @@
     def landed(ref, r):
         transfer(ref, ref, sibling, 0, r).wait_recv()
 
+    own = pltpu.make_async_copy(tok, X.at[0, 0, 0], lsem.at[0])
+    own.start()
     barrier = pltpu.get_barrier_semaphore()
 
     def greet(device):
@@ -113,8 +115,6 @@
     for e in far_first:
         greet(((z + e) % nz, ch_of(y, x, 1)))
 
-    own = pltpu.make_async_copy(tok, X.at[0, 0, 0], lsem.at[0])
-    own.start()
     for i, ref in enumerate((f1, f2)):
         pltpu.make_async_copy(ref, F.at[i], lsem.at[1]).start()
     for part, k in enumerate((2, 0, 1)):
@@ -187,6 +187,13 @@
         c = chip_of(dy, dx)
         weight = jnp.concatenate([Wv[part, c] for part in range(lo, hi)], axis=1)
         return jnp.dot(tile, weight, preferred_element_type=F32)
+
+    def half_terms(dy, dx, which, lo, hi):
+        c = chip_of(dy, dx)
+        owner = core if which == 0 else 1 - core
+        rows = pl.ds(pl.multiple_of(owner * B, B), B)
+        weight = jnp.concatenate([Wv[part, c, rows, :] for part in range(lo, hi)], axis=1)
+        return jnp.dot(X[dy, dx, which], weight, preferred_element_type=F32)
 
     def forward(g, e, s, r):
         lo, hi = groups[g]
@@ -243,6 +250,9 @@
     for dy in early:
         for dx in early:
             total += terms(dy, dx, 0, 3)
+    rest = [(dy, dx) for dy in range(1, q) for dx in range(1, q) if dy in late or dx in late]
+    for dy, dx in rest:
+        total += half_terms(dy, dx, 0, 0, 3)
     acc[...] = total
     for ref, r in last_fwd:
         landed(ref, r)
@@ -252,10 +262,9 @@
         pl.semaphore_wait(column_ready, 1)
 
 
-    rest = [(dy, dx) for dy in range(1, q) for dx in range(1, q) if dy in late or dx in late]
     total = acc[:, 0:B]
     for dy, dx in rest:
-        total += terms(dy, dx, 0, 1)
+        total += half_terms(dy, dx, 1, 0, 1)
     S0[...] = jnp.transpose(total).astype(BF16).reshape(nz, cz, B)
     s, value_in = out_of(S0.at[0 : nz - 1]), fresh("receive")
     for e in far_first:
@@ -265,7 +274,7 @@
     for part in range(2):
         total = acc[:, part * B + B : part * B + 2 * B]
         for dy, dx in rest:
-            total += terms(dy, dx, part + 1, part + 2)
+            total += half_terms(dy, dx, 1, part + 1, part + 2)
         S1[part] = jnp.transpose(total).astype(BF16).reshape(nz, cz, B)
         s, r = out_of(S1.at[part, 0 : nz - 1]), fresh("receive")
         for e in far_first:

time: 39.2 us -> 39.3 us (level)
  no operation moved by 1% of the time
where the time goes in v6:
time: 39.3 us; the launch traced here: 39.2 us
  Pallas kernels  38.5 us (98%)
  between operations  0.64 us (2%)
    pallas_call x1, Pallas kernels, per_device(): pl.pallas_call(functools.partial(kernel, q, nz, copies), out_shape=shapes...  37.9 us

profile of v6, /device:TPU:1, one launch (start us, length us, event | category | flops | bytes accessed | tf_op | source)
XLA Modules:
  0.0 39.2 jit_solution(13962128119556099768)
XLA Ops:
  0.6 37.9 %shard_map.76 = (bf16[128,128]{1,0:T(8,128)(2,1)S(1)}, f32[64,128]{1,0:T(8,128)S(1)}, f32[64,128]{1,0:T(8,128)S(1)}) custom-call(bf16[128,128]{1,0:T(8,128)(2,1)} %tok.1, bf16[3,16,256,128]{3,2,1,0:T(8,128)(2,1)} %bitcast.1, bf16[128,4096]{1,0:T(8,128)(2,1)} %wo.1, bf16[2,1536]{1,0:T(2,128)(2,1)} %f1.1, bf16[2,1536]{1,0:T(2,128)(2,1)} %f2.1), custom_call_target="tpu_custom_call" | custom-call | tf_op jit(solution)/shard_map/pallas_call | solution.py:467
  38.5 0.6 %shard_map.77 = (bf16[128,128]{1,0:T(8,128)(2,1)}, f32[64,128]{1,0:T(8,128)}, f32[64,128]{1,0:T(8,128)}) custom-call(bf16[128,128]{1,0:T(8,128)(2,1)S(1)} %get-tuple-element.6.a, f32[64,128]{1,0:T(8,128)S(1)} %get-tuple-element.7.b, f32[64,128]{1,0:T(8,128)S(1)} %get-tuple-element.8.c), custom_call_target="tpu_custom_call" | custom-call | tf_op jit(solution)/shard_map/pallas_call | solution.py:477
